TPU v7x, 256 devices: a whole 4x4x8 slice. The times are simulated.
256 devices in a mesh: ctx: 32 (over x, z), uly: 8 (over y, core).
Axes of the slice: x: 4, y: 4, z: 8, core: 2. Of those that a mesh axis runs over, the one named last changes fastest.
Arguments:
- queries: bfloat16 [32768, 7168], P(('ctx', 'uly')), may hold values from -6 to 6
- keys: bfloat16 [32768, 1024], P(('ctx', 'uly')), may hold values from -6 to 6
- values: bfloat16 [32768, 1024], P(('ctx', 'uly')), may hold values from -30 to 30
- cotangent: bfloat16 [32768, 7168], P(('ctx', 'uly')), may hold values from -6 to 6
- norm_gain: float32 [7168], replicated, may hold values from 0.1 to 1.9
- owner_of_row: int32 [32768], P('ctx'), may hold values from 0 to 31, as said below
- arrival: int32 [32768], P('ctx'), may hold values from 0 to 2047, as said below
- doc_start: int32 [32768], P('ctx'), may hold values from 0 to 1023, as said below
Outputs:
- normed: bfloat16 [32768, 7168], P(('ctx', 'uly'))
- grad_queries: bfloat16 [32768, 7168], P(('ctx', 'uly'))
- grad_keys: bfloat16 [32768, 1024], P(('ctx', 'uly'))
- grad_values: bfloat16 [32768, 1024], P(('ctx', 'uly'))
- grad_gain: float32 [7168], replicated
Inputs may be any that keep to these rules, and one draw needn't show every extreme that they name: `owner_of_row`: each owner gets exactly 1024 rows in all and at most 64 rows of one group; some group sends exactly 64 rows to each owner. `arrival`: consistent with owner_of_row as the steps state; the values of one owner are distinct. `doc_start`: documents are runs of 1 to 512 slots within one owner; every owner holds one document of exactly 512 slots.
All inputs are finite; a program needn't handle non-finite values.
Results may differ from a plain program's by a relative error of at most 0.012.
Values may be sent and summed in bfloat16 or wider, within the bound.
No kernel may reach another device: no remote copies, remote signals or barrier semaphores. Data moves between devices by JAX's collectives and lax.ppermute only.
A program may use at most 192 MiB of HBM per device.

v0:
```python
import jax
import jax.numpy as jnp
from jax import lax
from jax.sharding import PartitionSpec as P

HEAD_DIMENSION = 128


def block_weights(query_blk, key_win, first_key, query_pos, key_pos, score_scale):
    scores = (
        jnp.einsum("qngd,knd->ngqk", query_blk, key_win, preferred_element_type=jnp.float32)
        * score_scale
    )
    allowed = (key_pos[None, :] >= first_key[:, None]) & (key_pos[None, :] <= query_pos[:, None])
    scores = jnp.where(allowed, scores, -jnp.inf)
    row_peak = jnp.max(scores, axis=-1, keepdims=True)
    log_total = row_peak + jnp.log(jnp.sum(jnp.exp(scores - row_peak), axis=-1, keepdims=True))
    return jnp.exp(scores - log_total)


def per_device(queries, keys, values, cotangent, norm_gain, owner_of_row, arrival, doc_start):
    row_count = queries.shape[0]
    uly_size = lax.axis_size("uly")
    ctx_size = lax.axis_size("ctx")
    group_rows = row_count * uly_size
    capacity = 2 * group_rows // ctx_size
    head_size = HEAD_DIMENSION
    kv_local = keys.shape[1] // uly_size // head_size
    heads_local = queries.shape[1] // uly_size // head_size
    group_extent = heads_local // kv_local
    feat_local = heads_local * head_size
    width_all = queries.shape[1]
    score_scale = head_size ** (-0.5)
    owner_ids = jnp.arange(ctx_size, dtype=jnp.int32)
    onehot = (owner_of_row[:, None] == owner_ids[None, :]).astype(jnp.int32)
    row_rank = jnp.sum((jnp.cumsum(onehot, axis=0) - onehot) * onehot, axis=1)
    position = owner_of_row * capacity + row_rank
    source_of = (
        jnp.full((ctx_size * capacity,), group_rows, jnp.int32)
        .at[position]
        .set(jnp.arange(group_rows, dtype=jnp.int32))
    )

    def pack_rows(matrix):
        padded = jnp.concatenate([matrix, jnp.zeros((1, matrix.shape[1]), matrix.dtype)], axis=0)
        return padded[source_of]

    def spread_rows(matrix):
        return (
            jnp.zeros((ctx_size * capacity, matrix.shape[1]), matrix.dtype).at[arrival].set(matrix)
        )

    query_g, key_g, value_g, cot_g = (
        lax.all_to_all(queries, "uly", split_axis=1, concat_axis=0, tiled=True),
        lax.all_to_all(keys, "uly", split_axis=1, concat_axis=0, tiled=True),
        lax.all_to_all(values, "uly", split_axis=1, concat_axis=0, tiled=True),
        lax.all_to_all(cotangent, "uly", split_axis=1, concat_axis=0, tiled=True),
    )
    query_r, key_r, value_r, cot_r = (
        lax.all_to_all(pack_rows(query_g), "ctx", split_axis=0, concat_axis=0, tiled=True),
        lax.all_to_all(pack_rows(key_g), "ctx", split_axis=0, concat_axis=0, tiled=True),
        lax.all_to_all(pack_rows(value_g), "ctx", split_axis=0, concat_axis=0, tiled=True),
        lax.all_to_all(pack_rows(cot_g), "ctx", split_axis=0, concat_axis=0, tiled=True),
    )
    query_head = query_r[arrival].reshape(group_rows, kv_local, group_extent, head_size)
    key_head = key_r[arrival].reshape(group_rows, kv_local, head_size)
    value_head = value_r[arrival].reshape(group_rows, kv_local, head_size)
    doc_most = min(512, group_rows // 2)
    block_rows = min(512, group_rows)
    blocks = []
    for row_start in range(0, group_rows, block_rows):
        blocks.append((row_start, min(max(row_start - doc_most, 0), group_rows - group_rows)))

    def block_probs(row_start, win_start):
        query_blk = query_head[row_start : row_start + block_rows]
        first_key = doc_start[row_start : row_start + block_rows]
        query_pos = row_start + jnp.arange(block_rows, dtype=jnp.int32)
        key_pos = win_start + jnp.arange(group_rows, dtype=jnp.int32)
        weights = block_weights(query_blk, key_head, first_key, query_pos, key_pos, score_scale)
        return (query_blk, key_head, value_head, weights, weights.astype(jnp.bfloat16))

    outputs = []
    for row_start, win_start in blocks:
        query_blk, key_win, value_win, weights, rounded = block_probs(row_start, win_start)
        result = jnp.einsum(
            "ngqk,knd->qngd", rounded, value_win, preferred_element_type=jnp.float32
        )
        outputs.append(result.astype(jnp.bfloat16).reshape(block_rows, feat_local))
    attended = jnp.concatenate(outputs, axis=0)
    cot_wide = cot_r[arrival].astype(jnp.float32)
    gain_local = lax.dynamic_slice_in_dim(norm_gain, lax.axis_index("uly") * feat_local, feat_local)
    attended_wide = attended.astype(jnp.float32)
    square_part = jnp.sum(attended_wide * attended_wide, axis=1)
    cross_part = jnp.sum(gain_local * cot_wide * attended_wide, axis=1)
    square_sum, cross_sum = lax.psum((square_part, cross_part), "uly")
    norm_root = jnp.sqrt(square_sum / width_all + 1e-06)[:, None]
    normed_o = (gain_local * attended_wide / norm_root).astype(jnp.bfloat16)
    attention_gradient = gain_local * cot_wide / norm_root - attended_wide * (
        cross_sum[:, None] / (width_all * norm_root**3)
    )
    attention_gradient = attention_gradient.astype(jnp.bfloat16)
    gain_part = jnp.sum(cot_wide * attended_wide / norm_root, axis=0)
    grad_h = attention_gradient.reshape(group_rows, kv_local, group_extent, head_size)
    key_gradient = jnp.zeros((group_rows, kv_local, head_size), jnp.float32)
    value_gradient = jnp.zeros((group_rows, kv_local, head_size), jnp.float32)
    query_parts = []
    for row_start, win_start in blocks:
        query_blk, key_win, value_win, weights, rounded = block_probs(row_start, win_start)
        cot_blk = grad_h[row_start : row_start + block_rows]
        grad_weights = jnp.einsum(
            "qngd,knd->ngqk", cot_blk, value_win, preferred_element_type=jnp.float32
        )
        centre = jnp.sum(weights * grad_weights, axis=-1, keepdims=True)
        grad_scores = (weights * (grad_weights - centre)).astype(jnp.bfloat16)
        grad_query = (
            jnp.einsum("ngqk,knd->qngd", grad_scores, key_win, preferred_element_type=jnp.float32)
            * score_scale
        )
        query_parts.append(grad_query.astype(jnp.bfloat16).reshape(block_rows, feat_local))
        key_term = (
            jnp.einsum("ngqk,qngd->knd", grad_scores, query_blk, preferred_element_type=jnp.float32)
            * score_scale
        )
        value_term = jnp.einsum(
            "ngqk,qngd->knd", rounded, cot_blk, preferred_element_type=jnp.float32
        )
        key_gradient = key_gradient.at[win_start : win_start + group_rows].add(key_term)
        value_gradient = value_gradient.at[win_start : win_start + group_rows].add(value_term)
    grad_query_o = jnp.concatenate(query_parts, axis=0)
    grad_key_o = key_gradient.astype(jnp.bfloat16).reshape(group_rows, kv_local * head_size)
    grad_value_o = value_gradient.astype(jnp.bfloat16).reshape(group_rows, kv_local * head_size)
    back_query, back_key, back_value, back_normed = (
        lax.all_to_all(spread_rows(grad_query_o), "ctx", split_axis=0, concat_axis=0, tiled=True),
        lax.all_to_all(spread_rows(grad_key_o), "ctx", split_axis=0, concat_axis=0, tiled=True),
        lax.all_to_all(spread_rows(grad_value_o), "ctx", split_axis=0, concat_axis=0, tiled=True),
        lax.all_to_all(spread_rows(normed_o), "ctx", split_axis=0, concat_axis=0, tiled=True),
    )
    rows_query, rows_key, rows_value, rows_normed = (
        lax.all_to_all(back_query[position], "uly", split_axis=0, concat_axis=1, tiled=True),
        lax.all_to_all(back_key[position], "uly", split_axis=0, concat_axis=1, tiled=True),
        lax.all_to_all(back_value[position], "uly", split_axis=0, concat_axis=1, tiled=True),
        lax.all_to_all(back_normed[position], "uly", split_axis=0, concat_axis=1, tiled=True),
    )
    owner_total = lax.psum(gain_part, "ctx")
    grad_gain = lax.all_gather(owner_total, "uly", axis=0, tiled=True)
    return (rows_normed, rows_query, rows_key, rows_value, grad_gain)


def solution(mesh):
    placed = (
        P(("ctx", "uly"), None),
        P(("ctx", "uly"), None),
        P(("ctx", "uly"), None),
        P(("ctx", "uly"), None),
        P(),
        P("ctx"),
        P("ctx"),
        P("ctx"),
    )
    return jax.shard_map(
        per_device,
        mesh=mesh,
        in_specs=placed,
        out_specs=(
            P(("ctx", "uly"), None),
            P(("ctx", "uly"), None),
            P(("ctx", "uly"), None),
            P(("ctx", "uly"), None),
            P(),
        ),
        check_vma=False,
    )
```

profile of v0, /device:TPU:1, one launch (start us, length us, event | category | flops | bytes accessed | tf_op | source)
XLA Modules:
  0.0 819.1 jit_solution(16652680510779996353)
XLA Ops:
  9.6 9.0 %reduce-window.6 = s32[32,8,128]{2,1,0:T(8,128)S(1)} reduce-window(s32[32,8,128]{2,1,0:T(8,128)S(1)} %fusion.83, s32[]{:T(128)} %constant.160.clone.1), window={size=1x1x128 pad=0_0x0_0x127_0}, to_apply=%region_0.0 | reduce-window | flops 4161536 | bytes 262148 | tf_op jit(solution)/shard_map/reduce-window
  32.0 8.1 gather_fusion.2
  40.0 10.4 %all-to-all-start.3 = ((bf16[32,64,128]{2,1,0:T(8,128)(2,1)}), bf16[32,64,128]{2,1,0:T(8,128)(2,1)S(1)}, u32[]{:S(2)}, u32[]{:S(2)}) async-start(bf16[32,64,128]{2,1,0:T(8,128)(2,1)} %bitcast.10), calls=%async_computation.3 | async-start | bytes 1048576 | tf_op jit(solution)/shard_map/all_to_all | solution.py:61
  75.7 11.1 %all-to-all-done.1 = bf16[32,64,128]{2,1,0:T(8,128)(2,1)S(1)} async-done(((bf16[32,64,128]{2,1,0:T(8,128)(2,1)}), bf16[32,64,128]{2,1,0:T(8,128)(2,1)S(1)}, u32[]{:S(2)}, u32[]{:S(2)}) %all-to-all-start.1) | async-done | bytes 524320 | tf_op jit(solution)/shard_map/all_to_all | solution.py:62
  86.8 8.5 %all-to-all-start.4 = ((bf16[128,8,896]{2,0,1:T(8,128)(2,1)}), bf16[128,8,896]{2,0,1:T(8,128)(2,1)S(1)}, u32[]{:S(2)}, u32[]{:S(2)}) async-start(bf16[128,8,896]{2,0,1:T(8,128)(2,1)} %bitcast.247), calls=%async_computation.4 | async-start | bytes 3670016 | tf_op jit(solution)/shard_map/all_to_all | solution.py:54
  98.2 20.5 %all-to-all-done.4 = bf16[128,8,896]{2,0,1:T(8,128)(2,1)S(1)} async-done(((bf16[128,8,896]{2,0,1:T(8,128)(2,1)}), bf16[128,8,896]{2,0,1:T(8,128)(2,1)S(1)}, u32[]{:S(2)}, u32[]{:S(2)}) %all-to-all-start.4) | async-done | bytes 1835040 | tf_op jit(solution)/shard_map/all_to_all | solution.py:54
  125.5 9.5 %gather_fusion.4 = bf16[2048,896]{1,0:T(8,128)(2,1)} fusion(bf16[1025,896]{1,0:T(8,128)(2,1)S(1)} %concatenate.28, s32[2048]{0:T(1024)S(1)} %fusion.84), kind=kCustom, calls=%fused_computation.4 | custom fusion | bytes 7348224 | tf_op jit(solution)/shard_map/gather | solution.py:46
  135.0 12.5 %all-to-all-done.8 = bf16[128,8,896]{2,0,1:T(8,128)(2,1)} async-done(((bf16[128,8,896]{2,0,1:T(8,128)(2,1)}), bf16[128,8,896]{2,0,1:T(8,128)(2,1)}, u32[]{:S(2)}, u32[]{:S(2)}) %all-to-all-start.8) | async-done | bytes 1835040 | tf_op jit(solution)/shard_map/all_to_all | solution.py:57
  154.3 9.6 %gather_fusion.7 = bf16[2048,896]{1,0:T(8,128)(2,1)} fusion(bf16[1025,896]{1,0:T(8,128)(2,1)S(1)} %concatenate.30, s32[2048]{0:T(1024)S(1)} %fusion.84), kind=kCustom, calls=%fused_computation.7 | custom fusion | bytes 7348224 | tf_op jit(solution)/shard_map/gather | solution.py:46
  163.9 70.3 %all-to-all-done.5 = bf16[32,64,896]{2,1,0:T(8,128)(2,1)} async-done(((bf16[32,64,896]{2,1,0:T(8,128)(2,1)}), bf16[32,64,896]{2,1,0:T(8,128)(2,1)}, u32[]{:S(2)}, u32[]{:S(2)}) %all-to-all-start.5) | async-done | bytes 3670048 | tf_op jit(solution)/shard_map/all_to_all | solution.py:60
  234.2 9.3 %all-to-all-start.9 = ((bf16[32,64,896]{2,1,0:T(8,128)(2,1)}), bf16[32,64,896]{2,1,0:T(8,128)(2,1)}, u32[]{:S(2)}, u32[]{:S(2)}) async-start(bf16[32,64,896]{2,1,0:T(8,128)(2,1)} %bitcast.250), calls=%async_computation.9 | async-start | bytes 7340032 | tf_op jit(solution)/shard_map/all_to_all | solution.py:63
  304.2 8.7 %fusion.41 = bf16[128,7,512]{2,0,1:T(8,128)(2,1)} fusion(f32[1,7,512,1024]{2,3,1,0:T(8,128)} %get-tuple-element.98, f32[7,512]{1,0:T(8,128)S(1)} %log_add_fusion, bf16[1024,128]{1,0:T(8,128)(2,1)S(1)} %gather_fusion.1), kind=kOutput, calls=%fused_computation.78 | convolution fusion | flops 947322880 | bytes 15874048 | tf_op jit(solution)/shard_map/ngqk,knd->qngd/dot_general | solution.py:85
  314.9 13.4 %psum.21 = f32[1024]{0:T(1024)S(1)} all-reduce(f32[1024]{0:T(1024)S(1)} %fusion.17), channel_id=1, replica_groups=mesh['ctx'=32,'uly'=8] {'uly'}, use_global_device_ids=true, to_apply=%region_9.10 | all-reduce | flops 1024 | bytes 8192 | tf_op jit(solution)/shard_map/psum | solution.py:95
  328.3 8.2 %gather_fusion.8 = bf16[1024,896]{1,0:T(8,128)(2,1)} fusion(bf16[2048,896]{1,0:T(8,128)(2,1)} %bitcast.41, s32[1024]{0:T(1024)S(1)} %copy-done.16), kind=kCustom, calls=%fused_computation.8 | custom fusion | bytes 3674112 | tf_op jit(solution)/shard_map/gather | solution.py:90
  340.7 13.7 %psum.22 = f32[1024]{0:T(1024)S(1)} all-reduce(f32[1024]{0:T(1024)S(1)} %get-tuple-element.86), channel_id=1, replica_groups=mesh['ctx'=32,'uly'=8] {'uly'}, use_global_device_ids=true, to_apply=%region_12.13 | all-reduce | flops 1024 | bytes 8192 | tf_op jit(solution)/shard_map/psum | solution.py:95
  369.3 10.4 %fusion = (f32[7,512]{1,0:T(8,128)}, f32[1024,512,7]{1,0,2:T(8,128)}) fusion(f32[1,7,512,1024]{2,3,1,0:T(8,128)} %get-tuple-element.98, f32[7,512]{1,0:T(8,128)S(1)} %copy-done.13, bf16[512,7,128]{0,2,1:T(8,128)(2,1)S(1)} %bitcast.265, bf16[1024,128]{1,0:T(8,128)(2,1)S(1)} %gather_fusion.1), kind=kOutput, calls=%fused_computation.21 | convolution fusion | flops 950530560 | bytes 30568448 | tf_op jit(solution)/shard_map/qngd,knd->ngqk/dot_general | solution.py:110
  381.9 10.5 %fusion.3 = (f32[7,512]{1,0:T(8,128)}, f32[1024,512,7]{1,0,2:T(8,128)}) fusion(f32[1,7,512,1024]{2,3,1,0:T(8,128)} %get-tuple-element.100, f32[7,512]{1,0:T(8,128)S(1)} %log_add_fusion.1, bf16[512,7,128]{0,2,1:T(8,128)(2,1)} %bitcast.262, bf16[1024,128]{1,0:T(8,128)(2,1)S(1)} %gather_fusion.1), kind=kOutput, calls=%fused_computation.26 | convolution fusion | flops 950530560 | bytes 30568448 | tf_op jit(solution)/shard_map/qngd,knd->ngqk/dot_general | solution.py:110
  404.5 8.8 %all-to-all-start.14 = ((bf16[32,64,128]{2,1,0:T(8,128)(2,1)}), bf16[32,64,128]{2,1,0:T(8,128)(2,1)S(1)}, u32[]{:S(2)}, u32[]{:S(2)}) async-start(bf16[32,64,128]{2,1,0:T(8,128)(2,1)} %bitcast.272), calls=%async_computation.14 | async-start | bytes 1048576 | tf_op jit(solution)/shard_map/all_to_all | solution.py:135
  413.4 11.1 %fusion.10 = bf16[7,512,1024]{1,2,0:T(8,128)(2,1)S(1)} fusion(f32[1024,512,7]{1,0,2:T(8,128)} %get-tuple-element.104, f32[1,7,512,1024]{2,3,1,0:T(8,128)} %get-tuple-element.100, f32[7,512]{1,0:T(8,128)} %get-tuple-element.103, f32[7,512]{1,0:T(8,128)S(1)} %log_add_fusion.1), kind=kLoop, calls=%fused_computation.37 | loop fusion | flops 14680064 | bytes 36728832 | tf_op jit(solution)/shard_map/reshape.146
  448.3 9.3 %all-to-all-start.12 = ((bf16[32,64,128]{2,1,0:T(8,128)(2,1)}), bf16[32,64,128]{2,1,0:T(8,128)(2,1)S(1)}, u32[]{:S(2)}, u32[]{:S(2)}) async-start(bf16[32,64,128]{2,1,0:T(8,128)(2,1)} %bitcast.273), calls=%async_computation.12 | async-start | bytes 1048576 | tf_op jit(solution)/shard_map/all_to_all | solution.py:134
  462.0 9.4 %all-to-all-done.12 = bf16[32,64,128]{2,1,0:T(8,128)(2,1)S(1)} async-done(((bf16[32,64,128]{2,1,0:T(8,128)(2,1)}), bf16[32,64,128]{2,1,0:T(8,128)(2,1)S(1)}, u32[]{:S(2)}, u32[]{:S(2)}) %all-to-all-start.12) | async-done | bytes 524320 | tf_op jit(solution)/shard_map/all_to_all | solution.py:134
  501.9 8.7 %scatter_custom_fusion.2 = bf16[2048,896]{1,0:T(8,128)(2,1)} fusion(s32[1024]{0:T(1024)} %get-tuple-element.96, bf16[512,896]{1,0:T(8,128)(2,1)S(1)} %copy.101, bf16[]{:T(256)} %constant.187, bf16[512,896]{1,0:T(8,128)(2,1)} %copy.100, bf16[]{:T(256)} %constant.159.clone.1), kind=kCustom, calls=%fused_computation.68 | custom fusion | flops 3670016 | bytes 5506048 | tf_op jit(solution)/shard_map/scatter | solution.py:50
  515.7 9.0 %scatter_custom_fusion.1 = bf16[2048,896]{1,0:T(8,128)(2,1)} fusion(s32[1024]{0:T(1024)} %get-tuple-element.96, f32[1024]{0:T(1024)S(1)} %copy-done.22, f32[896]{0:T(1024)S(1)} %copy-done.20, bf16[]{:T(256)} %constant.159.clone.1, bf16[512,896]{1,0:T(8,128)(2,1)S(1)} %copy.89, bf16[512,896]{1,0:T(8,128)(2,1)S(1)} %copy.88), kind=kCustom, calls=%fused_computation.64 | custom fusion | flops 6422528 | bytes 5513216 | tf_op jit(solution)/shard_map/scatter | solution.py:50
  524.7 73.6 %all-to-all-done.10 = bf16[32,64,896]{2,1,0:T(8,128)(2,1)} async-done(((bf16[32,64,896]{2,1,0:T(8,128)(2,1)}), bf16[32,64,896]{2,1,0:T(8,128)(2,1)}, u32[]{:S(2)}, u32[]{:S(2)}) %all-to-all-start.10) | async-done | bytes 3670048 | tf_op jit(solution)/shard_map/all_to_all | solution.py:133
  598.3 8.5 %all-to-all-start.6 = ((bf16[32,64,896]{2,1,0:T(8,128)(2,1)}), bf16[32,64,896]{2,1,0:T(8,128)(2,1)}, u32[]{:S(2)}, u32[]{:S(2)}) async-start(bf16[32,64,896]{2,1,0:T(8,128)(2,1)} %bitcast.253), calls=%async_computation.6 | async-start | bytes 7340032 | tf_op jit(solution)/shard_map/all_to_all | solution.py:136
  606.8 8.2 %gather_fusion.9 = bf16[1024,896]{1,0:T(8,128)(2,1)} fusion(bf16[2048,896]{1,0:T(8,128)(2,1)} %bitcast.60, s32[1024]{0:T(1024)S(1)} %copy-done.17), kind=kCustom, calls=%fused_computation.9 | custom fusion | bytes 3674112 | tf_op jit(solution)/shard_map/gather | solution.py:139
  615.1 73.2 %all-to-all-done.6 = bf16[32,64,896]{2,1,0:T(8,128)(2,1)} async-done(((bf16[32,64,896]{2,1,0:T(8,128)(2,1)}), bf16[32,64,896]{2,1,0:T(8,128)(2,1)}, u32[]{:S(2)}, u32[]{:S(2)}) %all-to-all-start.6) | async-done | bytes 3670048 | tf_op jit(solution)/shard_map/all_to_all | solution.py:136
  688.3 9.6 %all-to-all-start.11 = ((bf16[8,128,896]{2,1,0:T(8,128)(2,1)}), bf16[8,128,896]{2,1,0:T(8,128)(2,1)S(1)}, u32[]{:S(2)}, u32[]{:S(2)}) async-start(bf16[8,128,896]{2,1,0:T(8,128)(2,1)} %bitcast.61), calls=%async_computation.11 | async-start | bytes 3670016 | tf_op jit(solution)/shard_map/all_to_all | solution.py:139
  697.9 8.2 %gather_fusion.6 = bf16[1024,896]{1,0:T(8,128)(2,1)} fusion(bf16[2048,896]{1,0:T(8,128)(2,1)} %bitcast.33, s32[1024]{0:T(1024)S(1)} %copy-done.17), kind=kCustom, calls=%fused_computation.6 | custom fusion | bytes 3674112 | tf_op jit(solution)/shard_map/gather | solution.py:142
  706.1 15.3 %all-to-all-done.11 = bf16[8,128,896]{2,1,0:T(8,128)(2,1)S(1)} async-done(((bf16[8,128,896]{2,1,0:T(8,128)(2,1)}), bf16[8,128,896]{2,1,0:T(8,128)(2,1)S(1)}, u32[]{:S(2)}, u32[]{:S(2)}) %all-to-all-start.11) | async-done | bytes 1835040 | tf_op jit(solution)/shard_map/all_to_all | solution.py:139
  726.5 57.5 %psum.23 = f32[896]{0:T(1024)S(1)} all-reduce(f32[896]{0:T(1024)S(1)} %copy-done.23), channel_id=1, replica_groups=mesh['ctx'=32,'uly'=8] {'ctx'}, use_global_device_ids=true, to_apply=%region_19.20 | all-reduce | flops 896 | bytes 7168 | tf_op jit(solution)/shard_map/psum | solution.py:144
  784.1 27.3 %all-gather = f32[8,1,896]{2,1,0:T(1,128)S(1)} all-gather(f32[1,1,896]{2,1,0:T(1,128)S(1)} %reshape.547), channel_id=1, replica_groups=mesh['ctx'=32,'uly'=8] {'uly'}, dimensions={0}, use_global_device_ids=true | all-gather | bytes 32256 | tf_op jit(solution)/shard_map/all_gather | solution.py:145
  (148 shorter events, 236.1 us)
Async XLA Ops:
  2.3 19.2 %all-to-all-start.2 = ((bf16[128,8,128]{2,0,1:T(8,128)(2,1)}), bf16[128,8,128]{2,0,1:T(8,128)(2,1)S(1)}, u32[]{:S(2)}, u32[]{:S(2)}) async-start(bf16[128,8,128]{2,0,1:T(8,128)(2,1)} %copy_bitcast_fusion.4), calls=%async_computation.2 | async-start | bytes 524288 | tf_op jit(solution)/shard_map/all_to_all | solution.py:55
  21.5 18.5 %all-to-all-start = ((bf16[128,8,128]{2,0,1:T(8,128)(2,1)}), bf16[128,8,128]{2,0,1:T(8,128)(2,1)S(1)}, u32[]{:S(2)}, u32[]{:S(2)}) async-start(bf16[128,8,128]{2,0,1:T(8,128)(2,1)} %copy_bitcast_fusion.5), calls=%async_computation | async-start | bytes 524288 | tf_op jit(solution)/shard_map/all_to_all | solution.py:56
  40.0 25.3 %all-to-all-start.3 = ((bf16[32,64,128]{2,1,0:T(8,128)(2,1)}), bf16[32,64,128]{2,1,0:T(8,128)(2,1)S(1)}, u32[]{:S(2)}, u32[]{:S(2)}) async-start(bf16[32,64,128]{2,1,0:T(8,128)(2,1)} %bitcast.10), calls=%async_computation.3 | async-start | bytes 1048576 | tf_op jit(solution)/shard_map/all_to_all | solution.py:61
  65.3 21.5 %all-to-all-start.1 = ((bf16[32,64,128]{2,1,0:T(8,128)(2,1)}), bf16[32,64,128]{2,1,0:T(8,128)(2,1)S(1)}, u32[]{:S(2)}, u32[]{:S(2)}) async-start(bf16[32,64,128]{2,1,0:T(8,128)(2,1)} %bitcast.5), calls=%async_computation.1 | async-start | bytes 1048576 | tf_op jit(solution)/shard_map/all_to_all | solution.py:62
  86.8 32.0 %all-to-all-start.4 = ((bf16[128,8,896]{2,0,1:T(8,128)(2,1)}), bf16[128,8,896]{2,0,1:T(8,128)(2,1)S(1)}, u32[]{:S(2)}, u32[]{:S(2)}) async-start(bf16[128,8,896]{2,0,1:T(8,128)(2,1)} %bitcast.247), calls=%async_computation.4 | async-start | bytes 3670016 | tf_op jit(solution)/shard_map/all_to_all | solution.py:54
  118.8 28.7 %all-to-all-start.8 = ((bf16[128,8,896]{2,0,1:T(8,128)(2,1)}), bf16[128,8,896]{2,0,1:T(8,128)(2,1)}, u32[]{:S(2)}, u32[]{:S(2)}) async-start(bf16[128,8,896]{2,0,1:T(8,128)(2,1)} %bitcast.246), calls=%async_computation.8 | async-start | bytes 3670016 | tf_op jit(solution)/shard_map/all_to_all | solution.py:57
  147.5 86.7 %all-to-all-start.5 = ((bf16[32,64,896]{2,1,0:T(8,128)(2,1)}), bf16[32,64,896]{2,1,0:T(8,128)(2,1)}, u32[]{:S(2)}, u32[]{:S(2)}) async-start(bf16[32,64,896]{2,1,0:T(8,128)(2,1)} %bitcast.251), calls=%async_computation.5 | async-start | bytes 7340032 | tf_op jit(solution)/shard_map/all_to_all | solution.py:60
  234.2 10.7 %copy-start.25 = (s32[1024]{0:T(1024)S(1)}, s32[1024]{0:T(1024)}, u32[]{:S(2)}) copy-start(s32[1024]{0:T(1024)} %param.31) | copy-start | bytes 12292
  234.2 10.7 %copy-start.24 = (s32[1024]{0:T(1024)S(1)}, s32[1024]{0:T(1024)}, u32[]{:S(2)}) copy-start(s32[1024]{0:T(1024)} %param.30) | copy-start | bytes 12292
  234.2 94.1 %all-to-all-start.9 = ((bf16[32,64,896]{2,1,0:T(8,128)(2,1)}), bf16[32,64,896]{2,1,0:T(8,128)(2,1)}, u32[]{:S(2)}, u32[]{:S(2)}) async-start(bf16[32,64,896]{2,1,0:T(8,128)(2,1)} %bitcast.250), calls=%async_computation.9 | async-start | bytes 7340032 | tf_op jit(solution)/shard_map/all_to_all | solution.py:63
  245.5 9.2 %copy-start.15 = (s32[1024]{0:T(1024)}, s32[1024]{0:T(1024)S(1)}, u32[]{:S(2)}) copy-start(s32[1024]{0:T(1024)S(1)} %get-tuple-element.95) | copy-start | bytes 12292
  312.9 15.4 %copy-start.16 = (s32[1024]{0:T(1024)S(1)}, s32[1024]{0:T(1024)}, u32[]{:S(2)}) copy-start(s32[1024]{0:T(1024)} %copy-done.15) | copy-start | bytes 12292
  328.3 26.1 %copy-start.21 = (f32[1024]{0:T(1024)}, f32[1024]{0:T(1024)S(1)}, u32[]{:S(2)}) copy-start(f32[1024]{0:T(1024)S(1)} %add_sqrt_fusion) | copy-start | bytes 12292
  381.9 10.5 %copy-start.6 = (bf16[512,896]{0,1:T(8,128)(2,1)S(1)}, bf16[512,896]{0,1:T(8,128)(2,1)}, u32[]{:S(2)}) copy-start(bf16[512,896]{0,1:T(8,128)(2,1)} %copy.92) | copy-start | bytes 2752516
  404.5 43.8 %all-to-all-start.14 = ((bf16[32,64,128]{2,1,0:T(8,128)(2,1)}), bf16[32,64,128]{2,1,0:T(8,128)(2,1)S(1)}, u32[]{:S(2)}, u32[]{:S(2)}) async-start(bf16[32,64,128]{2,1,0:T(8,128)(2,1)} %bitcast.272), calls=%async_computation.14 | async-start | bytes 1048576 | tf_op jit(solution)/shard_map/all_to_all | solution.py:135
  413.3 11.2 %slice-start = ((s8[14680064]{0:T(1024)(128)(4,1)}), s8[4194304]{0:T(1024)(128)(4,1)S(1)}, s32[]{:S(2)}) async-start(s8[14680064]{0:T(1024)(128)(4,1)} %bitcast.248), calls=%async_computation.16 | async-start | bytes 8388608
  413.3 12.0 %slice-start.1 = ((s8[14680064]{0:T(1024)(128)(4,1)}), s8[4194304]{0:T(1024)(128)(4,1)S(1)}, s32[]{:S(2)}) async-start(s8[14680064]{0:T(1024)(128)(4,1)} %bitcast.248), calls=%async_computation.17 | async-start | bytes 8388608
  413.4 15.7 %slice-start.2 = ((s8[14680064]{0:T(1024)(128)(4,1)}), s8[4194304]{0:T(1024)(128)(4,1)S(1)}, s32[]{:S(2)}) async-start(s8[14680064]{0:T(1024)(128)(4,1)} %bitcast.248), calls=%async_computation.18 | async-start | bytes 8388608
  413.4 16.4 %slice-start.3 = ((s8[14680064]{0:T(1024)(128)(4,1)}), s8[2097152]{0:T(1024)(128)(4,1)S(1)}, s32[]{:S(2)}) async-start(s8[14680064]{0:T(1024)(128)(4,1)} %bitcast.248), calls=%async_computation.19 | async-start | bytes 4194304
  413.4 16.4 %copy-start.14 = (f32[7,512]{1,0:T(8,128)S(1)}, f32[7,512]{1,0:T(8,128)}, u32[]{:S(2)}) copy-start(f32[7,512]{1,0:T(8,128)} %copy-done.12) | copy-start | bytes 43012
  413.4 16.4 %copy-start.18 = (f32[7,512]{1,0:T(8,128)S(1)}, f32[7,512]{1,0:T(8,128)}, u32[]{:S(2)}) copy-start(f32[7,512]{1,0:T(8,128)} %get-tuple-element.101) | copy-start | bytes 43012
  424.5 14.9 %copy-start.3 = (bf16[7,512,1024]{1,2,0:T(8,128)(2,1)}, bf16[7,512,1024]{1,2,0:T(8,128)(2,1)S(1)}, u32[]{:S(2)}) copy-start(bf16[7,512,1024]{1,2,0:T(8,128)(2,1)S(1)} %fusion.10) | copy-start | bytes 22020100
  439.9 17.8 %copy-start.17 = (s32[1024]{0:T(1024)S(1)}, s32[1024]{0:T(1024)}, u32[]{:S(2)}) copy-start(s32[1024]{0:T(1024)} %get-tuple-element.87) | copy-start | bytes 12292
  443.1 36.2 %copy-start.10 = (bf16[1024,128]{1,0:T(8,128)(2,1)S(1)}, bf16[1024,128]{1,0:T(8,128)(2,1)}, u32[]{:S(2)}) copy-start(bf16[1024,128]{1,0:T(8,128)(2,1)} %gather_fusion.3) | copy-start | bytes 786436
  448.3 23.1 %all-to-all-start.12 = ((bf16[32,64,128]{2,1,0:T(8,128)(2,1)}), bf16[32,64,128]{2,1,0:T(8,128)(2,1)S(1)}, u32[]{:S(2)}, u32[]{:S(2)}) async-start(bf16[32,64,128]{2,1,0:T(8,128)(2,1)} %bitcast.273), calls=%async_computation.12 | async-start | bytes 1048576 | tf_op jit(solution)/shard_map/all_to_all | solution.py:134
  471.4 17.3 %all-to-all-start.15 = ((bf16[8,128,128]{2,1,0:T(8,128)(2,1)}), bf16[8,128,128]{2,1,0:T(8,128)(2,1)S(1)}, u32[]{:S(2)}, u32[]{:S(2)}) async-start(bf16[8,128,128]{2,1,0:T(8,128)(2,1)} %bitcast.79), calls=%async_computation.15 | async-start | bytes 524288 | tf_op jit(solution)/shard_map/all_to_all | solution.py:141
  488.7 21.8 %all-to-all-start.13 = ((bf16[8,128,128]{2,1,0:T(8,128)(2,1)}), bf16[8,128,128]{2,1,0:T(8,128)(2,1)}, u32[]{:S(2)}, u32[]{:S(2)}) async-start(bf16[8,128,128]{2,1,0:T(8,128)(2,1)} %bitcast.70), calls=%async_computation.13 | async-start | bytes 524288 | tf_op jit(solution)/shard_map/all_to_all | solution.py:140
  510.6 87.7 %all-to-all-start.10 = ((bf16[32,64,896]{2,1,0:T(8,128)(2,1)}), bf16[32,64,896]{2,1,0:T(8,128)(2,1)}, u32[]{:S(2)}, u32[]{:S(2)}) async-start(bf16[32,64,896]{2,1,0:T(8,128)(2,1)} %bitcast.252), calls=%async_computation.10 | async-start | bytes 7340032 | tf_op jit(solution)/shard_map/all_to_all | solution.py:133
  598.3 90.0 %all-to-all-start.6 = ((bf16[32,64,896]{2,1,0:T(8,128)(2,1)}), bf16[32,64,896]{2,1,0:T(8,128)(2,1)}, u32[]{:S(2)}, u32[]{:S(2)}) async-start(bf16[32,64,896]{2,1,0:T(8,128)(2,1)} %bitcast.253), calls=%async_computation.6 | async-start | bytes 7340032 | tf_op jit(solution)/shard_map/all_to_all | solution.py:136
  688.3 33.1 %all-to-all-start.11 = ((bf16[8,128,896]{2,1,0:T(8,128)(2,1)}), bf16[8,128,896]{2,1,0:T(8,128)(2,1)S(1)}, u32[]{:S(2)}, u32[]{:S(2)}) async-start(bf16[8,128,896]{2,1,0:T(8,128)(2,1)} %bitcast.61), calls=%async_computation.11 | async-start | bytes 3670016 | tf_op jit(solution)/shard_map/all_to_all | solution.py:139
  706.1 20.4 %copy-start.23 = (f32[896]{0:T(1024)S(1)}, f32[896]{0:T(1024)}, u32[]{:S(2)}) copy-start(f32[896]{0:T(1024)} %get-tuple-element.85) | copy-start | bytes 10756
  721.4 93.9 %all-to-all-start.7 = ((bf16[8,128,896]{2,1,0:T(8,128)(2,1)}), bf16[8,128,896]{2,1,0:T(8,128)(2,1)}, u32[]{:S(2)}, u32[]{:S(2)}) async-start(bf16[8,128,896]{2,1,0:T(8,128)(2,1)} %bitcast.34), calls=%async_computation.7 | async-start | bytes 3670016 | tf_op jit(solution)/shard_map/all_to_all | solution.py:142
  (14 other events, 80.5 us)
where the time goes:
time: 826 us; the launch traced here: 819 us
  waiting for transfers between devices  293 us (35%)
  local copies, waits for them, and re-layouts  140 us (17%)
  starting transfers between devices  117 us (14%)
  blocking collectives  112 us (14%)
  matrix products  84.4 us (10%)
  other arithmetic  72.1 us (9%)
    all_to_all x1, waiting for transfers between devices, per_device(): lax.all_to_all(spread_rows(grad_query_o), 'ctx', split_axis=0, concat_axi...  73.6 us
    all_to_all x1, waiting for transfers between devices, per_device(): lax.all_to_all(spread_rows(normed_o), 'ctx', split_axis=0, concat_axis=0,...  73.2 us
    all_to_all x1, waiting for transfers between devices, per_device(): lax.all_to_all(pack_rows(query_g), 'ctx', split_axis=0, concat_axis=0, ti...  70.3 us
    psum x1, blocking collectives, per_device(): owner_total = lax.psum(gain_part, 'ctx')  57.5 us
    gather x4, local copies, waits for them, and re-layouts, pack_rows(): return padded[source_of]  35.2 us
    another operation x5, other arithmetic  27.4 us
    all_gather x1, blocking collectives, per_device(): grad_gain = lax.all_gather(owner_total, 'uly', axis=0, tiled=True)  27.3 us
    psum x2, blocking collectives, per_device(): square_sum, cross_sum = lax.psum((square_part, cross_part), 'uly')  27.1 us
  transfers between devices with their start and end apart: 16, of which 9 were waited for; matrix products, arithmetic and copies ran while one was open for 27% of the time, Pallas kernels for 0%

commit v1 on v0

v1 whole, which is shorter than its diff:
```python
import functools
import math

import jax
import jax.numpy as jnp
from jax import lax
from jax.experimental import pallas as pl
from jax.experimental.pallas import tpu as pltpu
from jax.sharding import PartitionSpec as P

HEAD = 128
BLOCK = 256
DOC_MAX = 512
HIDDEN = -1e30
VMEM_BYTES = 56 * 1024 * 1024
F32 = jnp.float32
BF16 = jnp.bfloat16


def params(grid_axes):
    return pltpu.CompilerParams(
        dimension_semantics=("arbitrary",) * grid_axes, vmem_limit_bytes=VMEM_BYTES
    )


def whole(shape):
    return pl.BlockSpec(shape, lambda i: (0,) * len(shape))


def row_block(cols, rows=BLOCK):
    return pl.BlockSpec((rows, cols), lambda i: (i, 0))


def as_column(row):
    return jnp.transpose(jnp.broadcast_to(row, (8, row.shape[1])))[:, 0:1]


def dot(a, b):
    return lax.dot_general(a, b, (((1,), (0,)), ((), ())), preferred_element_type=F32)


def dot_nt(a, b):
    return lax.dot_general(a, b, (((1,), (1,)), ((), ())), preferred_element_type=F32)


def cost(flops, nbytes, exps=0):
    return pl.CostEstimate(flops=int(flops), bytes_accessed=int(nbytes), transcendentals=int(exps))


def spread_kernel(target_ref, x_ref, out_ref):
    first = pl.program_id(0) * BLOCK
    place = first + lax.broadcasted_iota(jnp.int32, (BLOCK, target_ref.shape[1]), 0)
    hit = (place == target_ref[...]).astype(F32).astype(BF16)
    out_ref[...] = dot(hit, x_ref[...]).astype(BF16)


def spread_rows(x, target_row, out_rows):
    rows, cols = x.shape
    return pl.pallas_call(
        spread_kernel,
        grid=(out_rows // BLOCK,),
        in_specs=[whole((1, rows)), whole((rows, cols))],
        out_specs=row_block(cols),
        out_shape=jax.ShapeDtypeStruct((out_rows, cols), BF16),
        compiler_params=params(1),
        cost_estimate=cost(2 * rows * cols * out_rows, 2 * cols * (rows + out_rows)),
        name="spread_rows",
    )(target_row, x)


def take_kernel(source_ref, x_ref, out_ref):
    source = as_column(source_ref[...].astype(F32)).astype(jnp.int32)
    lane = lax.broadcasted_iota(jnp.int32, (BLOCK, x_ref.shape[0]), 1)
    hit = (lane == source).astype(F32).astype(BF16)
    out_ref[...] = dot(hit, x_ref[...]).astype(BF16)


def take_rows(x, source_row):
    rows, cols = x.shape
    out_rows = source_row.shape[1]
    return pl.pallas_call(
        take_kernel,
        grid=(out_rows // BLOCK,),
        in_specs=[pl.BlockSpec((1, BLOCK), lambda i: (0, i)), whole((rows, cols))],
        out_specs=row_block(cols),
        out_shape=jax.ShapeDtypeStruct((out_rows, cols), BF16),
        compiler_params=params(1),
        cost_estimate=cost(2 * rows * cols * out_rows, 2 * cols * (rows + out_rows)),
        name="take_rows",
    )(source_row, x)


def key_window(block):
    start = max(0, block * BLOCK - DOC_MAX)
    return start, (block + 1) * BLOCK - start


def window_bias(doc_ref, block):
    start, size = key_window(block)
    key_pos = start + lax.broadcasted_iota(jnp.int32, (size, BLOCK), 0)
    query_pos = block * BLOCK + lax.broadcasted_iota(jnp.int32, (size, BLOCK), 1)
    first_key = doc_ref[0:1, block * BLOCK : (block + 1) * BLOCK]
    return jnp.where((key_pos >= first_key) & (key_pos <= query_pos), 0.0, HIDDEN)


LOG2E = math.log2(math.e)


def forward_kernel(heads, doc_ref, kvq_ref, att_ref, stat_ref, value_t, bias_ref):
    rows = kvq_ref.shape[0]
    scale = HEAD ** (-0.5) * LOG2E
    value_t[...] = jnp.transpose(kvq_ref[:, HEAD : 2 * HEAD].astype(F32)).astype(BF16)
    for block in range(rows // BLOCK):
        start, size = key_window(block)
        q_rows = slice(block * BLOCK, (block + 1) * BLOCK)
        bias_ref[0:size, :] = window_bias(doc_ref, block)
        squares = jnp.zeros((1, BLOCK), F32)
        for head in range(heads):
            lanes = slice(head * HEAD, (head + 1) * HEAD)
            query = kvq_ref[q_rows, (head + 2) * HEAD : (head + 3) * HEAD]
            scores = dot_nt(kvq_ref[start : start + size, 0:HEAD], query) * scale + bias_ref[0:size, :]
            peak = jnp.max(scores, axis=0, keepdims=True)
            raised = jnp.exp2(scores - peak)
            total = jnp.sum(raised, axis=0, keepdims=True)
            weights = (raised * (1.0 / total)).astype(BF16)
            out_t = dot(value_t[:, start : start + size], weights)
            out = out_t.astype(BF16).astype(F32)
            squares = squares + jnp.sum(out * out, axis=0, keepdims=True)
            att_ref[q_rows, lanes] = jnp.transpose(out).astype(BF16)
            stat_ref[head : head + 1, q_rows] = peak + jnp.log2(total)
        stat_ref[7:8, q_rows] = squares


def forward_attention(kvq, doc_row):
    rows, cols = kvq.shape
    heads = cols // HEAD - 2
    pairs = rows * 576 * heads
    return pl.pallas_call(
        functools.partial(forward_kernel, heads),
        out_shape=(
            jax.ShapeDtypeStruct((rows, heads * HEAD), BF16),
            jax.ShapeDtypeStruct((8, rows), F32),
        ),
        scratch_shapes=[pltpu.VMEM((HEAD, rows), BF16), pltpu.VMEM((3 * BLOCK, BLOCK), F32)],
        compiler_params=pltpu.CompilerParams(vmem_limit_bytes=VMEM_BYTES),
        cost_estimate=cost(pairs * 16 * HEAD, 4 * rows * cols, pairs),
        name="forward_attention",
    )(doc_row, kvq)


def pack_normed_kernel(target_ref, att_ref, inv_ref, gain_ref, out_ref, normed):
    @pl.when(pl.program_id(0) == 0)
    def _():
        inv = as_column(inv_ref[...])
        normed[...] = (gain_ref[...] * att_ref[...].astype(F32) * inv).astype(BF16)

    spread_kernel(target_ref, normed, out_ref)


def pack_normed(att, inv_row, gain_row, target_row, out_rows):
    rows, cols = att.shape
    return pl.pallas_call(
        pack_normed_kernel,
        grid=(out_rows // BLOCK,),
        in_specs=[whole((1, rows)), whole((rows, cols)), whole((1, rows)), whole((1, cols))],
        out_specs=row_block(cols),
        out_shape=jax.ShapeDtypeStruct((out_rows, cols), BF16),
        scratch_shapes=[pltpu.VMEM((rows, cols), BF16)],
        compiler_params=params(1),
        cost_estimate=cost(2 * rows * cols * out_rows, 2 * cols * (rows + out_rows)),
        name="pack_normed",
    )(target_row, att, inv_row, gain_row)


def take_cotangent_kernel(source_ref, x_ref, att_ref, inv_ref, gain_ref, out_ref, cross_ref, part_ref):
    take_kernel(source_ref, x_ref, out_ref)
    product = out_ref[...].astype(F32) * att_ref[...].astype(F32)
    cross = jnp.sum(product * gain_ref[...], axis=1, keepdims=True)
    cross_ref[...] = jnp.transpose(jnp.broadcast_to(cross, (BLOCK, HEAD)))[0:1, :]

    @pl.when(pl.program_id(0) == 0)
    def _():
        part_ref[...] = jnp.zeros_like(part_ref)

    part_ref[...] += jnp.sum(product * as_column(inv_ref[...]), axis=0, keepdims=True)


def take_cotangent(received, source_row, att, inv_row, gain_row):
    rows, cols = att.shape
    lanes = pl.BlockSpec((1, BLOCK), lambda i: (0, i))
    return pl.pallas_call(
        take_cotangent_kernel,
        grid=(rows // BLOCK,),
        in_specs=[lanes, whole(received.shape), row_block(cols), lanes, whole((1, cols))],
        out_specs=(row_block(cols), lanes, whole((1, cols))),
        out_shape=(
            jax.ShapeDtypeStruct((rows, cols), BF16),
            jax.ShapeDtypeStruct((1, rows), F32),
            jax.ShapeDtypeStruct((1, cols), F32),
        ),
        compiler_params=params(1),
        cost_estimate=cost(2 * rows * cols * received.shape[0], 2 * cols * (3 * rows)),
        name="take_cotangent",
    )(source_row, received, att, inv_row, gain_row)


def backward_kernel(
    heads, doc_ref, kvq_ref, att_ref, cot_ref, stat_ref, inv_ref, cross_ref, gain_ref,
    out_ref, key_t, key_sum, value_sum, bias_ref,
):
    rows = kvq_ref.shape[0]
    width = heads * HEAD * 8
    scale = HEAD ** (-0.5)
    key_t[...] = jnp.transpose(kvq_ref[:, 0:HEAD].astype(F32)).astype(BF16)
    key_sum[...] = jnp.zeros_like(key_sum)
    value_sum[...] = jnp.zeros_like(value_sum)
    for block in range(rows // BLOCK):
        start, size = key_window(block)
        q_rows = slice(block * BLOCK, (block + 1) * BLOCK)
        keys = slice(start, start + size)
        bias_ref[0:size, :] = window_bias(doc_ref, block)
        inv = as_column(inv_ref[:, q_rows])
        shift = as_column(cross_ref[:, q_rows]) * (inv * inv * inv * (1.0 / width))
        for head in range(heads):
            lanes = slice(head * HEAD, (head + 1) * HEAD)
            wide = slice((head + 2) * HEAD, (head + 3) * HEAD)
            query = kvq_ref[q_rows, wide]
            grad = (
                gain_ref[:, lanes] * cot_ref[q_rows, lanes].astype(F32) * inv
                - att_ref[q_rows, lanes].astype(F32) * shift
            ).astype(BF16)
            scores = dot_nt(kvq_ref[keys, 0:HEAD], query) * (scale * LOG2E) + bias_ref[0:size, :]
            weights = jnp.exp2(scores - stat_ref[head : head + 1, q_rows])
            grad_weights = dot_nt(kvq_ref[keys, HEAD : 2 * HEAD], grad)
            centre = jnp.sum(weights * grad_weights, axis=0, keepdims=True)
            grad_scores = (weights * (grad_weights - centre)).astype(BF16)
            key_sum[keys, :] += dot(grad_scores, query)
            value_sum[keys, :] += dot(weights.astype(BF16), grad)
            grad_query = dot(key_t[:, keys], grad_scores) * scale
            out_ref[q_rows, wide] = jnp.transpose(grad_query).astype(BF16)
    out_ref[:, 0:HEAD] = (key_sum[...] * scale).astype(BF16)
    out_ref[:, HEAD : 2 * HEAD] = value_sum[...].astype(BF16)


def backward_attention(kvq, doc_row, att, cot, stats, inv_row, cross_row, gain_row):
    rows, cols = kvq.shape
    heads = cols // HEAD - 2
    pairs = rows * 576 * heads
    return pl.pallas_call(
        functools.partial(backward_kernel, heads),
        out_shape=jax.ShapeDtypeStruct((rows, cols), BF16),
        scratch_shapes=[
            pltpu.VMEM((HEAD, rows), BF16),
            pltpu.VMEM((rows, HEAD), F32),
            pltpu.VMEM((rows, HEAD), F32),
            pltpu.VMEM((3 * BLOCK, BLOCK), F32),
        ],
        compiler_params=pltpu.CompilerParams(vmem_limit_bytes=VMEM_BYTES),
        cost_estimate=cost(pairs * 30 * HEAD, 8 * rows * cols, pairs),
        name="backward_attention",
    )(doc_row, kvq, att, cot, stats, inv_row, cross_row, gain_row)


def sum_over(x, axis):
    size = lax.axis_size(axis)
    step = 1
    while step < size:
        x = x + lax.ppermute(x, axis, [(i, i ^ step) for i in range(size)])
        step *= 2
    return x


def shifted(axis, by):
    size = lax.axis_size(axis)
    return [(i, (i + by) % size) for i in range(size)]


def exchange(x, axis):
    return lax.all_to_all(x, axis, split_axis=0, concat_axis=0, tiled=True)


def per_device(queries, keys, values, cotangent, norm_gain, owner_of_row, arrival, doc_start):
    tok = queries.shape[0]
    uly = lax.axis_size("uly")
    ctx = lax.axis_size("ctx")
    rows = tok * uly
    capacity = 2 * rows // ctx
    sent = ctx * capacity
    width = queries.shape[1]
    feat = width // uly
    me = lax.axis_index("uly")

    with jax.named_scope("plan"):
        owner_ids = jnp.arange(ctx, dtype=jnp.int32)
        onehot = (owner_of_row[:, None] == owner_ids[None, :]).astype(BF16)
        row_ids = jnp.arange(rows, dtype=jnp.int32)
        earlier = (row_ids[None, :] < row_ids[:, None]).astype(BF16)
        before = dot(earlier, onehot)
        rank = jnp.sum(before * onehot.astype(F32), axis=1).astype(jnp.int32)
        position = (owner_of_row * capacity + rank)[None, :]
        by_shift = position.reshape(uly, tok)[(me - jnp.arange(uly)) % uly].reshape(1, rows)
        arrival_row = arrival[None, :]
        doc_row = doc_start[None, :]
        gain_row = lax.dynamic_slice_in_dim(norm_gain, me * feat, feat)[None, :]

    with jax.named_scope("rows_in"):
        kvq = jnp.concatenate(
            [
                keys.reshape(tok, uly, -1),
                values.reshape(tok, uly, -1),
                queries.reshape(tok, uly, feat),
            ],
            axis=2,
        ).transpose(1, 0, 2)
        kvq = exchange(kvq, "uly").reshape(rows, -1)
        cols = kvq.shape[1]
        kvq = spread_rows(kvq, position, sent)
        kvq = exchange(kvq.reshape(ctx, capacity, cols), "ctx").reshape(sent, cols)

    with jax.named_scope("cotangent_in"):
        blocks = []
        for shift in range(uly):
            block = lax.dynamic_slice_in_dim(cotangent, (me + shift) % uly * feat, feat, axis=1)
            blocks.append(lax.ppermute(block, "uly", shifted("uly", shift)) if shift else block)
        cot = spread_rows(jnp.concatenate(blocks, axis=0), by_shift, sent)
        cot = exchange(cot.reshape(ctx, capacity, feat), "ctx").reshape(sent, feat)

    with jax.named_scope("forward"):
        kvq = take_rows(kvq, arrival_row)
        att, stats = forward_attention(kvq, doc_row)
        square_sum = sum_over(stats[7:8, :], "uly")
        inv_root = lax.rsqrt(square_sum / width + 1e-06)

    with jax.named_scope("normed_out"):
        normed = pack_normed(att, inv_root, gain_row, arrival_row, sent)
        normed = exchange(normed.reshape(ctx, capacity, feat), "ctx").reshape(sent, feat)

    with jax.named_scope("backward"):
        cot, cross, gain_part = take_cotangent(cot, arrival_row, att, inv_root, gain_row)
        cross = sum_over(cross, "uly")
        grads = backward_attention(kvq, doc_row, att, cot, stats, inv_root, cross, gain_row)

    with jax.named_scope("grads_out"):
        grads = spread_rows(grads, arrival_row, sent)
        grads, normed = lax.optimization_barrier((grads, normed))
        grads = exchange(grads.reshape(ctx, capacity, cols), "ctx").reshape(sent, cols)

    with jax.named_scope("normed_rows"):
        normed = take_rows(normed, position).reshape(uly, tok, feat)
        normed_out = jnp.zeros((tok, width), BF16)
        for shift in range(uly):
            block = lax.dynamic_index_in_dim(normed, (me + shift) % uly, 0, keepdims=False)
            block = lax.ppermute(block, "uly", shifted("uly", shift)) if shift else block
            normed_out = lax.dynamic_update_slice_in_dim(
                normed_out, block, (me - shift) % uly * feat, axis=1
            )

    with jax.named_scope("grad_rows"):
        grads, normed_out = lax.optimization_barrier((grads, normed_out))
        grads = take_rows(grads, position).reshape(uly, tok, cols)
    with jax.named_scope("gain_out"):
        gain_part, grads = lax.optimization_barrier((gain_part, grads))
        gain_total = sum_over(gain_part, "ctx")
        grad_gain = jnp.zeros((1, width), F32)
        for shift in range(uly):
            block = lax.ppermute(gain_total, "uly", shifted("uly", shift)) if shift else gain_total
            grad_gain = lax.dynamic_update_slice_in_dim(
                grad_gain, block, (me - shift) % uly * feat, axis=1
            )

    with jax.named_scope("grad_cols"):
        grads = exchange(grads, "uly").transpose(1, 0, 2)
        grad_keys = grads[:, :, 0:HEAD].reshape(tok, -1)
        grad_values = grads[:, :, HEAD : 2 * HEAD].reshape(tok, -1)
        grad_queries = grads[:, :, 2 * HEAD :].reshape(tok, width)
    return normed_out, grad_queries, grad_keys, grad_values, grad_gain.reshape(width)


def solution(mesh):
    split = P(("ctx", "uly"), None)
    plan = P("ctx")
    return jax.shard_map(
        per_device,
        mesh=mesh,
        in_specs=(split, split, split, split, P(), plan, plan, plan),
        out_specs=(split, split, split, split, P()),
        check_vma=False,
    )
```

time: 826 us -> 528 us (0.64)
  Pallas kernels: 0 us -> 126 us
  blocking collectives: 112 us -> 0 us
  local copies, waits for them, and re-layouts: 140 us -> 28.3 us
  matrix products: 84.4 us -> 0.54 us
  other arithmetic: 72.1 us -> 5.07 us
  waiting for transfers between devices: 293 us -> 267 us
  starting transfers between devices: 117 us -> 92.3 us
    pallas_call x0 -> x10, Pallas kernels: none -> 126 us  [the longest x1 31 us: forward_attention(): pl.pallas_call(functools.partial(forward_kernel, heads), out_shape=(jax.S...]
    psum x3 -> x0, blocking collectives: 84.6 us -> none  [the longest x1 57.5 us: per_device(): owner_total = lax.psum(gain_part, 'ctx')]
    dot_general x12 -> x1, matrix products: 84.4 us -> 0.54 us  [dot(): lax.dot_general(a, b, (((1,), (0,)), ((), ())), preferred_element_type=F32)]
    all_to_all x16 -> x6, waiting for transfers between devices: 293 us -> 210 us  [exchange(): return lax.all_to_all(x, axis, split_axis=0, concat_axis=0, tiled=True)]
    gather x12 -> x1, local copies, waits for them, and re-layouts: 83.2 us -> 1.14 us  [per_device(): position.reshape(uly, tok)[(me - jnp.arange(uly)) % uly].reshape(1, rows)]
    all_to_all x16 -> x6, starting transfers between devices: 117 us -> 53.5 us  [exchange(): return lax.all_to_all(x, axis, split_axis=0, concat_axis=0, tiled=True)]
    ppermute x0 -> x32, waiting for transfers between devices: none -> 57 us  [the longest x14 28.7 us: per_device(): lax.ppermute(block, 'uly', shifted('uly', shift))]
    ppermute x0 -> x32, starting transfers between devices: none -> 38.7 us  [the longest x14 16 us: per_device(): lax.ppermute(block, 'uly', shifted('uly', shift))]
  transfers between devices with their start and end apart: 16 -> 38, of which waited for: 9 -> 22; matrix products, arithmetic and copies ran while one was open for 27% -> 5% of each run, Pallas kernels for 0% -> 21%
where the time goes in v1:
time: 528 us; the launch traced here: 520 us
  waiting for transfers between devices  267 us (51%)
  Pallas kernels  126 us (24%)
  starting transfers between devices  92.3 us (17%)
  local copies, waits for them, and re-layouts  28.3 us (5%)
    all_to_all x6, waiting for transfers between devices, exchange(): return lax.all_to_all(x, axis, split_axis=0, concat_axis=0, tiled=True)  210 us
    all_to_all x6, starting transfers between devices, exchange(): return lax.all_to_all(x, axis, split_axis=0, concat_axis=0, tiled=True)  53.5 us
    pallas_call x1, Pallas kernels, forward_attention(): pl.pallas_call(functools.partial(forward_kernel, heads), out_shape=(jax.S...  31 us
    pallas_call x3, Pallas kernels, take_rows(): pl.pallas_call(take_kernel, grid=(out_rows // BLOCK,), in_specs=[pl.Block...  29.4 us
    ppermute x14, waiting for transfers between devices, per_device(): lax.ppermute(block, 'uly', shifted('uly', shift))  28.7 us
    ppermute x11, waiting for transfers between devices, sum_over(): x = x + lax.ppermute(x, axis, [(i, i ^ step) for i in range(size)])  28.3 us
    pallas_call x3, Pallas kernels, spread_rows(): pl.pallas_call(spread_kernel, grid=(out_rows // BLOCK,), in_specs=[whole(...  27 us
    pallas_call x1, Pallas kernels, backward_attention(): pl.pallas_call(functools.partial(backward_kernel, heads), out_shape=jax.S...  19.7 us
  transfers between devices with their start and end apart: 38, of which 22 were waited for; matrix products, arithmetic and copies ran while one was open for 5% of the time, Pallas kernels for 21%

profile of v1, /device:TPU:1, one launch (start us, length us, event | category | flops | bytes accessed | tf_op | source)
XLA Modules:
  0.0 520.4 jit_solution(13772777270618857226)
XLA Ops:
  4.3 6.9 %all-to-all-start = ((bf16[8,128,1152]{2,1,0:T(8,128)(2,1)}), bf16[8,128,1152]{2,1,0:T(8,128)(2,1)S(1)}, u32[]{:S(2)}, u32[]{:S(2)}) async-start(bf16[8,128,1152]{2,1,0:T(8,128)(2,1)} %maximum_bitcast_fusion), calls=%async_computation | async-start | bytes 4718592 | tf_op jit(solution)/shard_map/rows_in/all_to_all | solution.py:279
  12.3 28.0 %all-to-all-done = bf16[8,128,1152]{2,1,0:T(8,128)(2,1)S(1)} async-done(((bf16[8,128,1152]{2,1,0:T(8,128)(2,1)}), bf16[8,128,1152]{2,1,0:T(8,128)(2,1)S(1)}, u32[]{:S(2)}, u32[]{:S(2)}) %all-to-all-start) | async-done | bytes 2359328 | tf_op jit(solution)/shard_map/rows_in/all_to_all | solution.py:279
  41.7 9.4 %spread_rows.3 = bf16[2048,1152]{1,0:T(8,128)(2,1)} custom-call(s32[1,1024]{1,0:T(1,128)} %bitcast.77, bf16[1024,1152]{1,0:T(8,128)(2,1)} %bitcast.72), custom_call_target="tpu_custom_call" | custom-call | flops 4831838208 | bytes 7077888 | tf_op jit(solution)/shard_map/rows_in/spread_rows/pallas_call | solution.py:59
  51.1 10.5 %all-to-all-start.1 = ((bf16[32,64,1152]{2,1,0:T(8,128)(2,1)}), bf16[32,64,1152]{2,1,0:T(8,128)(2,1)}, u32[]{:S(2)}, u32[]{:S(2)}) async-start(bf16[32,64,1152]{2,1,0:T(8,128)(2,1)} %bitcast.68), calls=%async_computation.1 | async-start | bytes 9437184 | tf_op jit(solution)/shard_map/rows_in/all_to_all | solution.py:279
  67.7 2.6 collective-permute-start.4
  72.7 14.8 %collective-permute-done.1 = bf16[128,896]{1,0:T(8,128)(2,1)S(1)} collective-permute-done((bf16[128,896]{1,0:T(8,128)(2,1)S(1)}, bf16[128,896]{1,0:T(8,128)(2,1)S(1)}, u32[]{:S(2)}, u32[]{:S(2)}) %collective-permute-start.1) | collective-permute-done | bytes 229408 | tf_op jit(solution)/shard_map/cotangent_in/ppermute | solution.py:324
  94.0 8.2 %spread_rows.4 = bf16[2048,896]{1,0:T(8,128)(2,1)} custom-call(s32[1,1024]{1,0:T(1,128)} %bitcast.83, bf16[1024,896]{1,0:T(8,128)(2,1)} %constant_dynamic-update-slice_fusion.x_ref), custom_call_target="tpu_custom_call" | custom-call | flops 3758096384 | bytes 5505024 | tf_op jit(solution)/shard_map/cotangent_in/spread_rows/pallas_call | solution.py:59
  102.2 63.9 %all-to-all-done.1 = bf16[32,64,1152]{2,1,0:T(8,128)(2,1)} async-done(((bf16[32,64,1152]{2,1,0:T(8,128)(2,1)}), bf16[32,64,1152]{2,1,0:T(8,128)(2,1)}, u32[]{:S(2)}, u32[]{:S(2)}) %all-to-all-start.1) | async-done | bytes 4718624 | tf_op jit(solution)/shard_map/rows_in/all_to_all | solution.py:279
  166.1 9.9 %all-to-all-start.2 = ((bf16[32,64,896]{2,1,0:T(8,128)(2,1)}), bf16[32,64,896]{2,1,0:T(8,128)(2,1)}, u32[]{:S(2)}, u32[]{:S(2)}) async-start(bf16[32,64,896]{2,1,0:T(8,128)(2,1)} %bitcast.69), calls=%async_computation.2 | async-start | bytes 7340032 | tf_op jit(solution)/shard_map/cotangent_in/all_to_all | solution.py:279
  176.0 10.5 %take_rows.3.kvq_ref = bf16[1024,1152]{1,0:T(8,128)(2,1)} custom-call(s32[1,1024]{1,0:T(1,128)} %bitcast.86, bf16[2048,1152]{1,0:T(8,128)(2,1)} %bitcast.6.x_ref), custom_call_target="tpu_custom_call" | custom-call | flops 4831838208 | bytes 7077888 | tf_op jit(solution)/shard_map/forward/take_rows/pallas_call | solution.py:81
  186.5 31.0 %forward_attention.1 = (bf16[1024,896]{1,0:T(8,128)(2,1)}, f32[8,1024]{1,0:T(8,128)}) custom-call(s32[1,1024]{1,0:T(1,128)} %bitcast.84, bf16[1024,1152]{1,0:T(8,128)(2,1)} %take_rows.3.kvq_ref), custom_call_target="tpu_custom_call" | custom-call | flops 8455716864 | bytes 4718592 | tf_op jit(solution)/shard_map/forward/forward_attention/pallas_call | solution.py:138
  221.4 2.6 collective-permute-done.8
  229.0 8.8 %pack_normed.1 = bf16[2048,896]{1,0:T(8,128)(2,1)} custom-call(s32[1,1024]{1,0:T(1,128)} %bitcast.87, bf16[1024,896]{1,0:T(8,128)(2,1)} %get-tuple-element.16.att_ref, f32[1,1024]{1,0:T(1,128)} %add_rsqrt_fusion.inv_ref, f32[1,896]{1,0:T(1,128)} %broadcast_in_dim.28.gain_ref), custom_call_target="tpu_custom_call" | custom-call | flops 3758096384 | bytes 5505024 | tf_op jit(solution)/shard_map/normed_out/pack_normed/pallas_call | solution.py:162
  237.8 19.8 %all-to-all-done.2 = bf16[32,64,896]{2,1,0:T(8,128)(2,1)} async-done(((bf16[32,64,896]{2,1,0:T(8,128)(2,1)}), bf16[32,64,896]{2,1,0:T(8,128)(2,1)}, u32[]{:S(2)}, u32[]{:S(2)}) %all-to-all-start.2) | async-done | bytes 3670048 | tf_op jit(solution)/shard_map/cotangent_in/all_to_all | solution.py:279
  257.6 9.1 %all-to-all-start.3 = ((bf16[32,64,896]{2,1,0:T(8,128)(2,1)}), bf16[32,64,896]{2,1,0:T(8,128)(2,1)}, u32[]{:S(2)}, u32[]{:S(2)}) async-start(bf16[32,64,896]{2,1,0:T(8,128)(2,1)} %bitcast.70), calls=%async_computation.3 | async-start | bytes 7340032 | tf_op jit(solution)/shard_map/normed_out/all_to_all | solution.py:279
  266.7 10.6 %take_cotangent.1 = (bf16[1024,896]{1,0:T(8,128)(2,1)}, f32[1,1024]{1,0:T(1,128)}, f32[1,896]{1,0:T(1,128)}) custom-call(s32[1,1024]{1,0:T(1,128)} %bitcast.88, bf16[2048,896]{1,0:T(8,128)(2,1)} %bitcast.11.x_ref, bf16[1024,896]{1,0:T(8,128)(2,1)} %get-tuple-element.16.att_ref, f32[1,1024]{1,0:T(1,128)} %add_rsqrt_fusion.inv_ref, ...), custom_call_target="tpu_custom_call" | custom-call | flops 3758096384 | bytes 5505024 | tf_op jit(solution)/shard_map/backward/take_cotangent/pallas_call | solution.py:191
  280.4 2.6 collective-permute-done.11
  284.2 3.2 collective-permute-done.12
  287.9 19.7 %backward_attention.1.x_ref = bf16[1024,1152]{1,0:T(8,128)(2,1)} custom-call(s32[1,1024]{1,0:T(1,128)} %bitcast.85, bf16[1024,1152]{1,0:T(8,128)(2,1)} %take_rows.3.kvq_ref, bf16[1024,896]{1,0:T(8,128)(2,1)} %get-tuple-element.16.att_ref, bf16[1024,896]{1,0:T(8,128)(2,1)} %get-tuple-element.18.cot_ref, f32[8,1024]{1,0:T(8,128)} %get-tuple-element.17.stat_ref, ...), custom_call_target="tpu_custom_call" | custom-call | flops 15854469120 | bytes 9437184 | tf_op jit(solution)/shard_map/backward/backward_attention/pallas_call | solution.py:249
  307.6 9.4 %spread_rows.5 = bf16[2048,1152]{1,0:T(8,128)(2,1)} custom-call(s32[1,1024]{1,0:T(1,128)} %bitcast.89, bf16[1024,1152]{1,0:T(8,128)(2,1)} %backward_attention.1.x_ref), custom_call_target="tpu_custom_call" | custom-call | flops 4831838208 | bytes 7077888 | tf_op jit(solution)/shard_map/grads_out/spread_rows/pallas_call | solution.py:59
  317.0 31.2 %all-to-all-done.3 = bf16[32,64,896]{2,1,0:T(8,128)(2,1)} async-done(((bf16[32,64,896]{2,1,0:T(8,128)(2,1)}), bf16[32,64,896]{2,1,0:T(8,128)(2,1)}, u32[]{:S(2)}, u32[]{:S(2)}) %all-to-all-start.3) | async-done | bytes 3670048 | tf_op jit(solution)/shard_map/normed_out/all_to_all | solution.py:279
  348.2 9.1 %all-to-all-start.4 = ((bf16[32,64,1152]{2,1,0:T(8,128)(2,1)}), bf16[32,64,1152]{2,1,0:T(8,128)(2,1)}, u32[]{:S(2)}, u32[]{:S(2)}) async-start(bf16[32,64,1152]{2,1,0:T(8,128)(2,1)} %bitcast.67), calls=%async_computation.4 | async-start | bytes 9437184 | tf_op jit(solution)/shard_map/grads_out/all_to_all | solution.py:279
  357.3 8.7 %take_rows.4 = bf16[1024,896]{1,0:T(8,128)(2,1)} custom-call(s32[1,1024]{1,0:T(1,128)} %bitcast.78, bf16[2048,896]{1,0:T(8,128)(2,1)} %bitcast.13.x_ref), custom_call_target="tpu_custom_call" | custom-call | flops 3758096384 | bytes 5505024 | tf_op jit(solution)/shard_map/normed_rows/take_rows/pallas_call | solution.py:81
  369.5 3.2 collective-permute-start.15
  384.2 8.2 %collective-permute-done.16 = bf16[128,896]{1,0:T(8,128)(2,1)S(1)} collective-permute-done((bf16[128,896]{1,0:T(8,128)(2,1)S(1)}, bf16[128,896]{1,0:T(8,128)(2,1)S(1)}, u32[]{:S(2)}, u32[]{:S(2)}) %collective-permute-start.16) | collective-permute-done | bytes 229408 | tf_op jit(solution)/shard_map/normed_rows/ppermute | solution.py:353
  395.3 66.6 %all-to-all-done.4 = bf16[32,64,1152]{2,1,0:T(8,128)(2,1)} async-done(((bf16[32,64,1152]{2,1,0:T(8,128)(2,1)}), bf16[32,64,1152]{2,1,0:T(8,128)(2,1)}, u32[]{:S(2)}, u32[]{:S(2)}) %all-to-all-start.4) | async-done | bytes 4718624 | tf_op jit(solution)/shard_map/grads_out/all_to_all | solution.py:279
  461.9 10.1 %take_rows.5 = bf16[1024,1152]{1,0:T(8,128)(2,1)} custom-call(s32[1,1024]{1,0:T(1,128)} %bitcast.79, bf16[2048,1152]{1,0:T(8,128)(2,1)} %bitcast.15.x_ref), custom_call_target="tpu_custom_call" | custom-call | flops 4831838208 | bytes 7077888 | tf_op jit(solution)/shard_map/grad_rows/take_rows/pallas_call | solution.py:81
  472.1 8.1 %all-to-all-start.5 = ((bf16[8,128,1152]{2,1,0:T(8,128)(2,1)}), bf16[8,128,1152]{2,1,0:T(8,128)(2,1)S(1)}, u32[]{:S(2)}, u32[]{:S(2)}) async-start(bf16[8,128,1152]{2,1,0:T(8,128)(2,1)} %bitcast.71), calls=%async_computation.5 | async-start | bytes 4718592 | tf_op jit(solution)/shard_map/grad_cols/all_to_all | solution.py:279
  483.5 2.8 collective-permute-done.21
  487.4 5.3 %collective-permute-done.22 = f32[1,896]{1,0:T(1,128)S(1)} collective-permute-done((f32[1,896]{1,0:T(1,128)S(1)}, f32[1,896]{1,0:T(1,128)S(1)}, u32[]{:S(2)}, u32[]{:S(2)}) %collective-permute-start.22) | collective-permute-done | bytes 3616 | tf_op jit(solution)/shard_map/gain_out/ppermute | solution.py:268
  492.8 2.7 collective-permute-done.23
  499.6 6.8 %collective-permute-start.25 = (f32[1,896]{1,0:T(1,128)S(1)}, f32[1,896]{1,0:T(1,128)S(1)}, u32[]{:S(2)}, u32[]{:S(2)}) collective-permute-start(f32[1,896]{1,0:T(1,128)S(1)} %get-tuple-element.28), channel_id=1, source_target_pairs={{0,1},{1,2},{2,3},{3,4},{4,5},{5,6},{6,7},{7,0},{8,9},{9,10},{10,1... | collective-permute-start | bytes 10760 | tf_op jit(solution)/shard_map/gain_out/ppermute | solution.py:366
  (133 shorter events, 74.9 us)
Async XLA Ops:
  4.3 36.1 %all-to-all-start = ((bf16[8,128,1152]{2,1,0:T(8,128)(2,1)}), bf16[8,128,1152]{2,1,0:T(8,128)(2,1)S(1)}, u32[]{:S(2)}, u32[]{:S(2)}) async-start(bf16[8,128,1152]{2,1,0:T(8,128)(2,1)} %maximum_bitcast_fusion), calls=%async_computation | async-start | bytes 4718592 | tf_op jit(solution)/shard_map/rows_in/all_to_all | solution.py:279
  51.1 115.0 %all-to-all-start.1 = ((bf16[32,64,1152]{2,1,0:T(8,128)(2,1)}), bf16[32,64,1152]{2,1,0:T(8,128)(2,1)}, u32[]{:S(2)}, u32[]{:S(2)}) async-start(bf16[32,64,1152]{2,1,0:T(8,128)(2,1)} %bitcast.68), calls=%async_computation.1 | async-start | bytes 9437184 | tf_op jit(solution)/shard_map/rows_in/all_to_all | solution.py:279
  62.8 8.7 %collective-permute-start = (bf16[128,896]{1,0:T(8,128)(2,1)}, bf16[128,896]{1,0:T(8,128)(2,1)S(1)}, u32[]{:S(2)}, u32[]{:S(2)}) collective-permute-start(bf16[128,896]{1,0:T(8,128)(2,1)} %get-tuple-element.43), channel_id=1, source_target_pairs={{0,1},{1,2},{2,3},{3,4},{4,5},{5,6},{6,7},{7,0},{8,9},{9,10},{10,1... | collective-permute-start | bytes 688136 | tf_op jit(solution)/shard_map/cotangent_in/ppermute | solution.py:324
  64.1 23.3 %collective-permute-start.1 = (bf16[128,896]{1,0:T(8,128)(2,1)S(1)}, bf16[128,896]{1,0:T(8,128)(2,1)S(1)}, u32[]{:S(2)}, u32[]{:S(2)}) collective-permute-start(bf16[128,896]{1,0:T(8,128)(2,1)S(1)} %get-tuple-element.42), channel_id=1, source_target_pairs={{0,2},{1,3},{2,4},{3,5},{4,6},{5,7},{6,0},{7,1},{8,10},{9,11},{10,... | collective-permute-start | bytes 688136 | tf_op jit(solution)/shard_map/cotangent_in/ppermute | solution.py:324
  64.1 24.0 %collective-permute-start.2 = (bf16[128,896]{1,0:T(8,128)(2,1)S(1)}, bf16[128,896]{1,0:T(8,128)(2,1)S(1)}, u32[]{:S(2)}, u32[]{:S(2)}) collective-permute-start(bf16[128,896]{1,0:T(8,128)(2,1)S(1)} %get-tuple-element.41), channel_id=1, source_target_pairs={{0,3},{1,4},{2,5},{3,6},{4,7},{5,0},{6,1},{7,2},{8,11},{9,12},{10,... | collective-permute-start | bytes 688136 | tf_op jit(solution)/shard_map/cotangent_in/ppermute | solution.py:324
  66.2 22.6 %collective-permute-start.3 = (bf16[128,896]{1,0:T(8,128)(2,1)S(1)}, bf16[128,896]{1,0:T(8,128)(2,1)S(1)}, u32[]{:S(2)}, u32[]{:S(2)}) collective-permute-start(bf16[128,896]{1,0:T(8,128)(2,1)S(1)} %get-tuple-element.40), channel_id=1, source_target_pairs={{0,4},{1,5},{2,6},{3,7},{4,0},{5,1},{6,2},{7,3},{8,12},{9,13},{10,... | collective-permute-start | bytes 688136 | tf_op jit(solution)/shard_map/cotangent_in/ppermute | solution.py:324
  67.7 21.9 %collective-permute-start.4 = (bf16[128,896]{1,0:T(8,128)(2,1)S(1)}, bf16[128,896]{1,0:T(8,128)(2,1)S(1)}, u32[]{:S(2)}, u32[]{:S(2)}) collective-permute-start(bf16[128,896]{1,0:T(8,128)(2,1)S(1)} %get-tuple-element.39), channel_id=1, source_target_pairs={{0,5},{1,6},{2,7},{3,0},{4,1},{5,2},{6,3},{7,4},{8,13},{9,14},{10,... | collective-permute-start | bytes 688136 | tf_op jit(solution)/shard_map/cotangent_in/ppermute | solution.py:324
  71.5 18.8 %collective-permute-start.5 = (bf16[128,896]{1,0:T(8,128)(2,1)S(1)}, bf16[128,896]{1,0:T(8,128)(2,1)S(1)}, u32[]{:S(2)}, u32[]{:S(2)}) collective-permute-start(bf16[128,896]{1,0:T(8,128)(2,1)S(1)} %get-tuple-element.45), channel_id=1, source_target_pairs={{0,6},{1,7},{2,0},{3,1},{4,2},{5,3},{6,4},{7,5},{8,14},{9,15},{10,... | collective-permute-start | bytes 688136 | tf_op jit(solution)/shard_map/cotangent_in/ppermute | solution.py:324
  87.4 5.8 %collective-permute-start.6 = (bf16[128,896]{1,0:T(8,128)(2,1)S(1)}, bf16[128,896]{1,0:T(8,128)(2,1)S(1)}, u32[]{:S(2)}, u32[]{:S(2)}) collective-permute-start(bf16[128,896]{1,0:T(8,128)(2,1)S(1)} %get-tuple-element.38), channel_id=1, source_target_pairs={{0,7},{1,0},{2,1},{3,2},{4,3},{5,4},{6,5},{7,6},{8,15},{9,8},{10,9... | collective-permute-start | bytes 688136 | tf_op jit(solution)/shard_map/cotangent_in/ppermute | solution.py:324
  166.1 91.4 %all-to-all-start.2 = ((bf16[32,64,896]{2,1,0:T(8,128)(2,1)}), bf16[32,64,896]{2,1,0:T(8,128)(2,1)}, u32[]{:S(2)}, u32[]{:S(2)}) async-start(bf16[32,64,896]{2,1,0:T(8,128)(2,1)} %bitcast.69), calls=%async_computation.2 | async-start | bytes 7340032 | tf_op jit(solution)/shard_map/cotangent_in/all_to_all | solution.py:279
  224.0 4.4 collective-permute-start.9
  257.6 90.6 %all-to-all-start.3 = ((bf16[32,64,896]{2,1,0:T(8,128)(2,1)}), bf16[32,64,896]{2,1,0:T(8,128)(2,1)}, u32[]{:S(2)}, u32[]{:S(2)}) async-start(bf16[32,64,896]{2,1,0:T(8,128)(2,1)} %bitcast.70), calls=%async_computation.3 | async-start | bytes 7340032 | tf_op jit(solution)/shard_map/normed_out/all_to_all | solution.py:279
  283.0 4.4 collective-permute-start.12
  348.2 113.7 %all-to-all-start.4 = ((bf16[32,64,1152]{2,1,0:T(8,128)(2,1)}), bf16[32,64,1152]{2,1,0:T(8,128)(2,1)}, u32[]{:S(2)}, u32[]{:S(2)}) async-start(bf16[32,64,1152]{2,1,0:T(8,128)(2,1)} %bitcast.67), calls=%async_computation.4 | async-start | bytes 9437184 | tf_op jit(solution)/shard_map/grads_out/all_to_all | solution.py:279
  367.7 10.6 %collective-permute-start.13 = (bf16[128,896]{1,0:T(8,128)(2,1)S(1)}, bf16[128,896]{1,0:T(8,128)(2,1)S(1)}, u32[]{:S(2)}, u32[]{:S(2)}) collective-permute-start(bf16[128,896]{1,0:T(8,128)(2,1)S(1)} %get-tuple-element.37), channel_id=1, source_target_pairs={{0,1},{1,2},{2,3},{3,4},{4,5},{5,6},{6,7},{7,0},{8,9},{9,10},{10,1... | collective-permute-start | bytes 688136 | tf_op jit(solution)/shard_map/normed_rows/ppermute | solution.py:353
  369.0 12.8 %collective-permute-start.14 = (bf16[128,896]{1,0:T(8,128)(2,1)S(1)}, bf16[128,896]{1,0:T(8,128)(2,1)S(1)}, u32[]{:S(2)}, u32[]{:S(2)}) collective-permute-start(bf16[128,896]{1,0:T(8,128)(2,1)S(1)} %get-tuple-element.36), channel_id=1, source_target_pairs={{0,2},{1,3},{2,4},{3,5},{4,6},{5,7},{6,0},{7,1},{8,10},{9,11},{10,... | collective-permute-start | bytes 688136 | tf_op jit(solution)/shard_map/normed_rows/ppermute | solution.py:353
  369.5 14.0 %collective-permute-start.15 = (bf16[128,896]{1,0:T(8,128)(2,1)S(1)}, bf16[128,896]{1,0:T(8,128)(2,1)S(1)}, u32[]{:S(2)}, u32[]{:S(2)}) collective-permute-start(bf16[128,896]{1,0:T(8,128)(2,1)S(1)} %get-tuple-element.35), channel_id=1, source_target_pairs={{0,3},{1,4},{2,5},{3,6},{4,7},{5,0},{6,1},{7,2},{8,11},{9,12},{10,... | collective-permute-start | bytes 688136 | tf_op jit(solution)/shard_map/normed_rows/ppermute | solution.py:353
  372.7 19.7 %collective-permute-start.16 = (bf16[128,896]{1,0:T(8,128)(2,1)S(1)}, bf16[128,896]{1,0:T(8,128)(2,1)S(1)}, u32[]{:S(2)}, u32[]{:S(2)}) collective-permute-start(bf16[128,896]{1,0:T(8,128)(2,1)S(1)} %get-tuple-element.34), channel_id=1, source_target_pairs={{0,4},{1,5},{2,6},{3,7},{4,0},{5,1},{6,2},{7,3},{8,12},{9,13},{10,... | collective-permute-start | bytes 688136 | tf_op jit(solution)/shard_map/normed_rows/ppermute | solution.py:353
  372.7 20.5 %collective-permute-start.17 = (bf16[128,896]{1,0:T(8,128)(2,1)S(1)}, bf16[128,896]{1,0:T(8,128)(2,1)S(1)}, u32[]{:S(2)}, u32[]{:S(2)}) collective-permute-start(bf16[128,896]{1,0:T(8,128)(2,1)S(1)} %get-tuple-element.33), channel_id=1, source_target_pairs={{0,5},{1,6},{2,7},{3,0},{4,1},{5,2},{6,3},{7,4},{8,13},{9,14},{10,... | collective-permute-start | bytes 688136 | tf_op jit(solution)/shard_map/normed_rows/ppermute | solution.py:353
  378.3 15.6 %collective-permute-start.18 = (bf16[128,896]{1,0:T(8,128)(2,1)S(1)}, bf16[128,896]{1,0:T(8,128)(2,1)S(1)}, u32[]{:S(2)}, u32[]{:S(2)}) collective-permute-start(bf16[128,896]{1,0:T(8,128)(2,1)S(1)} %get-tuple-element.32), channel_id=1, source_target_pairs={{0,6},{1,7},{2,0},{3,1},{4,2},{5,3},{6,4},{7,5},{8,14},{9,15},{10,... | collective-permute-start | bytes 688136 | tf_op jit(solution)/shard_map/normed_rows/ppermute | solution.py:353
  381.8 12.8 %collective-permute-start.19 = (bf16[128,896]{1,0:T(8,128)(2,1)S(1)}, bf16[128,896]{1,0:T(8,128)(2,1)S(1)}, u32[]{:S(2)}, u32[]{:S(2)}) collective-permute-start(bf16[128,896]{1,0:T(8,128)(2,1)S(1)} %get-tuple-element.31), channel_id=1, source_target_pairs={{0,7},{1,0},{2,1},{3,2},{4,3},{5,4},{6,5},{7,6},{8,15},{9,8},{10,9... | collective-permute-start | bytes 688136 | tf_op jit(solution)/shard_map/normed_rows/ppermute | solution.py:353
  472.1 44.3 %all-to-all-start.5 = ((bf16[8,128,1152]{2,1,0:T(8,128)(2,1)}), bf16[8,128,1152]{2,1,0:T(8,128)(2,1)S(1)}, u32[]{:S(2)}, u32[]{:S(2)}) async-start(bf16[8,128,1152]{2,1,0:T(8,128)(2,1)} %bitcast.71), calls=%async_computation.5 | async-start | bytes 4718592 | tf_op jit(solution)/shard_map/grad_cols/all_to_all | solution.py:279
  482.7 3.6 collective-permute-start.21
  486.3 6.4 %collective-permute-start.22 = (f32[1,896]{1,0:T(1,128)S(1)}, f32[1,896]{1,0:T(1,128)S(1)}, u32[]{:S(2)}, u32[]{:S(2)}) collective-permute-start(f32[1,896]{1,0:T(1,128)S(1)} %add.303), channel_id=1, source_target_pairs={{0,32},{8,40},{16,48},{24,56},{32,0},{40,8},{48,16},{56,24},{64,96... | collective-permute-start | bytes 10760 | tf_op jit(solution)/shard_map/gain_out/ppermute | solution.py:268
  495.6 4.0 collective-permute-start.24
  499.6 11.9 %collective-permute-start.25 = (f32[1,896]{1,0:T(1,128)S(1)}, f32[1,896]{1,0:T(1,128)S(1)}, u32[]{:S(2)}, u32[]{:S(2)}) collective-permute-start(f32[1,896]{1,0:T(1,128)S(1)} %get-tuple-element.28), channel_id=1, source_target_pairs={{0,1},{1,2},{2,3},{3,4},{4,5},{5,6},{6,7},{7,0},{8,9},{9,10},{10,1... | collective-permute-start | bytes 10760 | tf_op jit(solution)/shard_map/gain_out/ppermute | solution.py:366
  506.4 5.9 %collective-permute-start.26 = (f32[1,896]{1,0:T(1,128)S(1)}, f32[1,896]{1,0:T(1,128)S(1)}, u32[]{:S(2)}, u32[]{:S(2)}) collective-permute-start(f32[1,896]{1,0:T(1,128)S(1)} %get-tuple-element.28), channel_id=1, source_target_pairs={{0,2},{1,3},{2,4},{3,5},{4,6},{5,7},{6,0},{7,1},{8,10},{9,11},{10,... | collective-permute-start | bytes 10760 | tf_op jit(solution)/shard_map/gain_out/ppermute | solution.py:366
  507.6 7.2 %collective-permute-start.27 = (f32[1,896]{1,0:T(1,128)S(1)}, f32[1,896]{1,0:T(1,128)S(1)}, u32[]{:S(2)}, u32[]{:S(2)}) collective-permute-start(f32[1,896]{1,0:T(1,128)S(1)} %get-tuple-element.28), channel_id=1, source_target_pairs={{0,3},{1,4},{2,5},{3,6},{4,7},{5,0},{6,1},{7,2},{8,11},{9,12},{10,... | collective-permute-start | bytes 10760 | tf_op jit(solution)/shard_map/gain_out/ppermute | solution.py:366
  509.2 5.9 %collective-permute-start.28 = (f32[1,896]{1,0:T(1,128)S(1)}, f32[1,896]{1,0:T(1,128)S(1)}, u32[]{:S(2)}, u32[]{:S(2)}) collective-permute-start(f32[1,896]{1,0:T(1,128)S(1)} %get-tuple-element.28), channel_id=1, source_target_pairs={{0,4},{1,5},{2,6},{3,7},{4,0},{5,1},{6,2},{7,3},{8,12},{9,13},{10,... | collective-permute-start | bytes 10760 | tf_op jit(solution)/shard_map/gain_out/ppermute | solution.py:366
  509.7 5.7 %collective-permute-start.29 = (f32[1,896]{1,0:T(1,128)S(1)}, f32[1,896]{1,0:T(1,128)S(1)}, u32[]{:S(2)}, u32[]{:S(2)}) collective-permute-start(f32[1,896]{1,0:T(1,128)S(1)} %get-tuple-element.28), channel_id=1, source_target_pairs={{0,5},{1,6},{2,7},{3,0},{4,1},{5,2},{6,3},{7,4},{8,13},{9,14},{10,... | collective-permute-start | bytes 10760 | tf_op jit(solution)/shard_map/gain_out/ppermute | solution.py:366
  511.5 4.3 collective-permute-start.30
  512.3 3.8 collective-permute-start.31
  (15 other events, 58.5 us)
